TPU v7x, 128 devices: a whole 4x4x4 slice. The times are simulated.
128 devices in a mesh: group: 8 (over x, core), member: 16 (over y, z).
Axes of the slice: x: 4, y: 4, z: 4, core: 2. Of those that a mesh axis runs over, the one named last changes fastest.
Arguments:
- root_front: float32 [8192, 8192], P('member', 'group'), may hold values from -6 to 6
- child_panels: bfloat16 [8, 4096, 4096], P('group', 'member'), may hold values from -1.75 to 1.75
- pivot_sizes: float32 [8, 4096], P('group'), may hold values from 0.02 to 4
- pivot_signs: int32 [8, 4096], P('group'), may hold values from 0 to 1
- child_blocks: int32 [8, 32], replicated, may hold values from 0 to 63, as said below
Outputs:
- updated_front: float32 [8192, 8192], P('member', 'group')
Inputs may be any that keep to these rules, and one draw needn't show every extreme that they name: Each row child_blocks[g] holds 32 distinct root blocks in increasing order, exactly 2 of them in each run of root blocks k * 4 to (k + 1) * 4 - 1.
All inputs are finite; a program needn't handle non-finite values.
Results may differ from a plain program's by a relative error of at most 0.0044.
Values may be sent and summed in bfloat16 or wider, within the bound.
A program may use at most 128 MiB of HBM per device.

v0:
```python
import jax
import jax.numpy as jnp
from jax import lax
from jax.sharding import PartitionSpec as P

B = 128
S = 8192


pivot_floor = 0.1
highest = lax.Precision.HIGHEST


def pair_product(left, right):
    return lax.dot_general(
        left, right, (((1,), (1,)), ((), ())), preferred_element_type=jnp.float32
    )


def local(root_front, child_panels, pivot_sizes, pivot_signs, child_blocks):
    members = lax.axis_size("member")
    groups = lax.axis_size("group")
    member_index = lax.axis_index("member")
    group_index = lax.axis_index("group")
    clipped = jnp.maximum(pivot_sizes[0], pivot_floor)
    sign_vals = (2 * pivot_signs[0] - 1).astype(jnp.float32)
    scaled = (child_panels[0].astype(jnp.float32) * jnp.sqrt(clipped)[None, :]).astype(jnp.bfloat16)
    signed = (scaled.astype(jnp.float32) * sign_vals[None, :]).astype(jnp.bfloat16)
    own_rows = scaled.shape[0]
    total_rows = own_rows * members
    child_count = total_rows // B
    keep_blocks = own_rows // B
    run_blocks = S // B // members
    row_strip = pair_product(signed, lax.all_gather(scaled, "member", axis=0, tiled=True))
    row_targets = (
        lax.dynamic_slice_in_dim(child_blocks, member_index * keep_blocks, keep_blocks, 1)
        - member_index * run_blocks
    )
    row_hot = (
        row_targets[:, :, None] == jnp.arange(run_blocks, dtype=jnp.int32)[None, None, :]
    ).astype(jnp.float32)
    own_blocks = lax.dynamic_index_in_dim(child_blocks, group_index, 0, keepdims=False)
    col_hot = (own_blocks[:, None] == jnp.arange(S // B, dtype=jnp.int32)[None, :]).astype(
        jnp.float32
    )
    strip_blocks = row_strip.reshape(own_rows, child_count, B)
    expanded = jnp.einsum("rab,ap->rpb", strip_blocks, col_hot, precision=highest).reshape(
        own_rows, S
    )
    arrived = lax.all_to_all(expanded, "group", split_axis=1, concat_axis=0, tiled=True)
    arrived = arrived.reshape(groups, keep_blocks, B, S // groups)
    assembled = jnp.einsum("gkic,gkp->pic", arrived, row_hot, precision=highest)
    assembled = assembled.reshape(root_front.shape[0], root_front.shape[1])
    return root_front - assembled


def solution(mesh):
    placed = (
        P("member", "group"),
        P("group", "member", None),
        P("group", None),
        P("group", None),
        P(),
    )
    return jax.shard_map(
        local, mesh=mesh, in_specs=placed, out_specs=P("member", "group"), check_vma=False
    )
```

profile of v0, /device:TPU:7, one launch (start us, length us, event | category | flops | bytes accessed | tf_op | source)
XLA Modules:
  0.0 374.5 jit_solution(5857047649839633765)
XLA Ops:
  6.5 0.0 copy-start.1
  6.5 0.0 copy-start.3
  6.5 0.0 copy-start.2
  6.5 0.0 all-gather.2.cloned.1.call-start
  6.5 0.9 maximum_sqrt_fusion
  7.5 3.4 fusion.4
  10.8 0.0 all-gather.2.cloned.1.call-update
  10.9 0.0 copy-done.3
  10.9 0.0 copy-done.2
  10.9 199.6 %all-gather.2.cloned.1.call-done = bf16[4096,4096]{1,0:T(8,128)(2,1)} async-done(((bf16[256,4096]{1,0:T(8,128)(2,1)}), bf16[4096,4096]{1,0:T(8,128)(2,1)}) %all-gather.2.cloned.1.call-update) | async-done | bytes 33554448 | tf_op jit(solution)/shard_map/all_gather | solution.py:34
  210.5 0.0 copy-done.1
  210.5 14.2 %fusion.11 = f32[256,32,128]{2,0,1:T(8,128)S(1)} fusion(bf16[32,128,4096]{2,1,0:T(8,128)(2,1)} %bitcast.35, bf16[1,256,4096]{2,1,0:T(8,128)(2,1)S(1)} %copy-done.1, f32[4096]{0:T(1024)S(1)} %bitcast.34, f32[4096]{0:T(1024)S(1)} %bitcast.33), kind=kOutput, calls=%fused_computation.12 | convolution fusion | flops 8596226048 | bytes 39878656 | tf_op jit(solution)/shard_map/dot_general | solution.py:15
  224.8 9.5 %fusion.7 = f32[256,64,128]{2,1,0:T(8,128)} fusion(f32[256,32,128]{2,0,1:T(8,128)S(1)} %fusion.11, s32[32]{0:T(128)S(1)} %dynamic-slice_bitcast_fusion), kind=kOutput, calls=%fused_computation.10 | convolution fusion | flops 805308416 | bytes 12583040 | tf_op jit(solution)/shard_map/rab,ap->rpb/dot_general | solution.py:47
  234.3 9.3 %all_to_all.12 = f32[256,8,1024]{2,1,0:T(8,128)} reshape(f32[256,64,128]{2,1,0:T(8,128)} %fusion.7) | data formatting | bytes 16777216 | tf_op jit(solution)/shard_map/all_to_all | solution.py:50
  243.6 11.5 %copy.8 = f32[256,8,1024]{2,0,1:T(8,128)} copy(f32[256,8,1024]{2,1,0:T(8,128)} %all_to_all.12) | data formatting | bytes 16777216 | tf_op jit(solution)/shard_map/all_to_all | solution.py:50
  255.0 5.9 %all-to-all-start = ((f32[256,8,1024]{2,0,1:T(8,128)}), f32[256,8,1024]{2,0,1:T(8,128)}, u32[]{:S(2)}, u32[]{:S(2)}) async-start(f32[256,8,1024]{2,0,1:T(8,128)} %copy.8), calls=%async_computation | async-start | bytes 16777216 | tf_op jit(solution)/shard_map/all_to_all | solution.py:50
  260.9 0.1 dynamic-slice_subtract_fusion
  261.0 0.1 copy.7
  261.1 92.0 %all-to-all-done = f32[256,8,1024]{2,0,1:T(8,128)} async-done(((f32[256,8,1024]{2,0,1:T(8,128)}), f32[256,8,1024]{2,0,1:T(8,128)}, u32[]{:S(2)}, u32[]{:S(2)}) %all-to-all-start) | async-done | bytes 8388640 | tf_op jit(solution)/shard_map/all_to_all | solution.py:50
  353.0 11.3 %fusion.16 = f32[4,128,1024]{2,0,1:T(4,128)S(1)} fusion(f32[8,2,128,1024]{3,2,1,0:T(8,128)} %bitcast.11, s32[8,2]{0,1:T(2,128)S(1)} %copy.7), kind=kOutput, calls=%fused_computation.16 | convolution fusion | flops 100663360 | bytes 10485824 | tf_op jit(solution)/shard_map/gkic,gkp->pic/dot_general | solution.py:52
  364.4 0.0 copy-start
  364.4 1.2 copy.10
  365.6 0.4 copy-done
  365.9 1.7 bitcast_subtract_fusion
  (2 shorter events, 0.0 us)
Async XLA Ops:
  6.5 204.0 %copy-start.1 = (bf16[1,256,4096]{2,1,0:T(8,128)(2,1)S(1)}, bf16[1,256,4096]{2,1,0:T(8,128)(2,1)}, u32[]{:S(2)}) copy-start(bf16[1,256,4096]{2,1,0:T(8,128)(2,1)} %param.6) | copy-start | bytes 6291460
  6.5 4.3 %copy-start.3 = (s32[8,32]{1,0:T(8,128)S(1)}, s32[8,32]{1,0:T(8,128)}, u32[]{:S(2)}) copy-start(s32[8,32]{1,0:T(8,128)} %param.9) | copy-start | bytes 3076
  6.5 4.4 %copy-start.2 = (s32[1,4096]{1,0:T(1,128)S(1)}, s32[1,4096]{1,0:T(1,128)}, u32[]{:S(2)}) copy-start(s32[1,4096]{1,0:T(1,128)} %param.8) | copy-start | bytes 49156
  6.5 204.0 %all-gather.2.cloned.1.call-start = ((), (), s32[]{:S(2)}) async-start(), calls=%async_computation.1 | async-start | bytes 35651584 | tf_op jit(solution)/shard_map/all_gather | solution.py:34
  255.0 98.0 %all-to-all-start = ((f32[256,8,1024]{2,0,1:T(8,128)}), f32[256,8,1024]{2,0,1:T(8,128)}, u32[]{:S(2)}, u32[]{:S(2)}) async-start(f32[256,8,1024]{2,0,1:T(8,128)} %copy.8), calls=%async_computation | async-start | bytes 16777216 | tf_op jit(solution)/shard_map/all_to_all | solution.py:50
  364.4 1.6 copy-start
Sparse Core Ops, SparseCore 0:
  11.0 199.5 all-gather.1
where the time goes:
time: 378 us; the launch traced here: 375 us
  waiting for transfers between devices  292 us (77%)
  matrix products  35 us (9%)
  local copies, waits for them, and re-layouts  22.4 us (6%)
  between operations  13.5 us (4%)
  other arithmetic  6.12 us (2%)
  starting transfers between devices  5.89 us (2%)
    all_gather x1, waiting for transfers between devices, local(): lax.all_gather(scaled, 'member', axis=0, tiled=True)  200 us
    all_to_all x1, waiting for transfers between devices, local(): lax.all_to_all(expanded, 'group', split_axis=1, concat_axis=0, tiled=True)  92 us
    all_to_all x2, local copies, waits for them, and re-layouts, local(): lax.all_to_all(expanded, 'group', split_axis=1, concat_axis=0, tiled=True)  20.8 us
    dot_general x1, matrix products, pair_product(): lax.dot_general(left, right, (((1,), (1,)), ((), ())), preferred_element_...  14.2 us
    dot_general x1, matrix products, local(): assembled = jnp.einsum('gkic,gkp->pic', arrived, row_hot, precision=highest)  11.3 us
    dot_general x1, matrix products, local(): jnp.einsum('rab,ap->rpb', strip_blocks, col_hot, precision=highest)  9.5 us
  transfers between devices with their start and end apart: 2, of which 2 were waited for; matrix products, arithmetic and copies ran while one was open for 0% of the time, Pallas kernels for 0%

commit v1 on v0

v1 whole, which is shorter than its diff:
```python
import jax
import jax.numpy as jnp
from jax import lax
from jax.experimental import pallas as pl
from jax.experimental.pallas import tpu as pltpu
from jax.sharding import PartitionSpec as P

B = 128
ROWS = 256
K = 4096
NC = 8
KC = K // NC
SIDE = 4
pivot_floor = 0.1

TRI = ((0, 0), (0, 1), (1, 0), (1, 1), (0, 2), (2, 0))
PAIRS = (
    (0, 0, False),
    (0, 1, True),
    (0, 2, True),
    (2, 1, True),
    (0, 3, True),
    (0, 4, False),
    (2, 4, True),
    (0, 5, False),
    (5, 1, True),
    (5, 4, False),
)


def dot_nt(left, right):
    return lax.dot_general(left, right, (((1,), (1,)), ((), ())), preferred_element_type=jnp.float32)


def meet_kernel(panel, sizes, signs, arrived, pan, acc, stage, load_sem, hop_send, hop_recv, tile_send, tile_recv):
    group = lax.axis_index("group")
    member = lax.axis_index("member")
    row, col = member // SIDE, member % SIDE
    turn = 1 - 2 * (group % 2)

    def at(offset):
        y = (row + turn * offset[0] + SIDE) % SIDE
        z = (col + turn * offset[1] + SIDE) % SIDE
        return y * SIDE + z

    to_z, to_y = at((0, -1)), at((-1, 0))

    def cols(k):
        return pl.ds(pl.multiple_of(k * KC, KC), KC)

    def load(k):
        return pltpu.make_async_copy(panel.at[0, :, cols(k)], pan.at[0, :, cols(k)], load_sem.at[k])

    def hop(src, dst, k, target):
        return pltpu.make_async_remote_copy(
            src_ref=pan.at[src, :, cols(k)],
            dst_ref=pan.at[dst, :, cols(k)],
            send_sem=hop_send.at[dst - 1, k],
            recv_sem=hop_recv.at[dst - 1, k],
            device_id={"group": group, "member": target},
            device_id_type=pl.DeviceIdType.MESH,
        )

    def hop_corner(k):
        return hop(2, 3, k, to_z) if k % 2 == 0 else hop(1, 3, k, to_y)

    def each(body):
        lax.fori_loop(0, NC, lambda k, c: (body(k), c)[1], 0)

    for k in range(NC):
        load(k).start()

    root = jnp.sqrt(jnp.maximum(sizes[...], pivot_floor))
    sign = (2 * signs[...] - 1).astype(jnp.float32).astype(jnp.bfloat16)
    sizes_root, sign_row = root, sign

    for k in range(NC):
        load(k).wait()
        s = slice(k * KC, (k + 1) * KC)
        pan[0, :, s] = (pan[0, :, s].astype(jnp.float32) * sizes_root[:, s]).astype(jnp.bfloat16)
        hop(0, 1, k, to_z).start()
        hop(0, 2, k, to_y).start()

    def signed(slot, k):
        s = (2 * signs[:, cols(k)] - 1).astype(jnp.float32).astype(jnp.bfloat16)
        return pan[slot, :, cols(k)] * s

    def accumulate(n, left, right, k):
        prod = dot_nt(left, pan[right, :, cols(k)])

        @pl.when(k == 0)
        def _():
            acc[n] = prod

        @pl.when(k > 0)
        def _():
            acc[n] += prod

    def send_copies():
        out = []
        slot = 0
        for n, (a, b, both) in enumerate(PAIRS):
            for r, c in ((a, b), (b, a)) if both else ((a, b),):
                row_at, col_at = at(TRI[r]), at(TRI[c])
                out.append((n, slot, r, c, (r, c) != (a, b), row_at, col_at))
                slot += 1
        return out

    copies = send_copies()

    def tile(slot, row_at, col_at):
        return pltpu.make_async_remote_copy(
            src_ref=stage.at[slot],
            dst_ref=arrived.at[group, col_at % 2],
            send_sem=tile_send.at[slot],
            recv_sem=tile_recv.at[group, col_at % 2],
            device_id={"group": col_at // 2, "member": row_at},
            device_id_type=pl.DeviceIdType.MESH,
        )

    def tile_here(slot, col_at):
        return pltpu.make_async_copy(stage.at[slot], arrived.at[group, col_at % 2], tile_recv.at[group, col_at % 2])

    def ship(n):
        for m, slot, r, c, flipped, row_at, col_at in copies:
            if m != n:
                continue
            value = acc[n]
            stage[slot] = (value.T if flipped else value).astype(jnp.bfloat16)
            if r == 0:
                here = col_at // 2 == group

                @pl.when(here)
                def _():
                    tile_here(slot, col_at).start()

                @pl.when(jnp.logical_not(here))
                def _():
                    tile(slot, row_at, col_at).start()
            else:
                tile(slot, row_at, col_at).start()

    def first(k):
        own = signed(0, k)
        accumulate(0, own, 0, k)
        hop(0, 1, k, to_z).wait_recv()
        hop(0, 2, k, to_y).wait_recv()
        accumulate(1, own, 1, k)
        accumulate(2, own, 2, k)
        accumulate(3, signed(2, k), 1, k)

    each(first)
    for k in range(NC):
        hop_corner(k).start()
    for k in range(NC):
        hop(1, 4, k, to_z).start()
        hop(2, 5, k, to_y).start()
    for n in range(4):
        ship(n)

    def corner(k):
        hop(2, 3, k, to_z).wait_recv()
        accumulate(4, signed(0, k), 3, k)

    each(corner)
    ship(4)

    def far(k):
        hop(1, 4, k, to_z).wait_recv()
        hop(2, 5, k, to_y).wait_recv()
        own = signed(0, k)
        accumulate(5, own, 4, k)
        accumulate(6, signed(2, k), 4, k)
        accumulate(7, own, 5, k)
        last = signed(5, k)
        accumulate(8, last, 1, k)
        accumulate(9, last, 4, k)

    each(far)
    for n in range(5, 10):
        ship(n)

    def drain(k):
        hop(0, 1, k, to_z).wait_send()
        hop(0, 2, k, to_y).wait_send()
        hop(2, 3, k, to_z).wait_send()
        hop(1, 4, k, to_z).wait_send()
        hop(2, 5, k, to_y).wait_send()

    each(drain)
    for _, slot, r, c, _, row_at, col_at in copies:
        if r == 0:

            @pl.when(col_at // 2 != group)
            def _():
                tile(slot, row_at, col_at).wait_send()
        else:
            tile(slot, row_at, col_at).wait_send()
    for g in range(8):
        for j in range(2):
            pltpu.make_async_copy(stage.at[0], arrived.at[g, j], tile_recv.at[g, j]).wait()


def meet(panel, sizes, signs):
    return pl.pallas_call(
        meet_kernel,
        out_shape=jax.ShapeDtypeStruct((8, 2, ROWS, ROWS), jnp.bfloat16),
        in_specs=[
            pl.BlockSpec(memory_space=pl.ANY),
            pl.BlockSpec(memory_space=pltpu.VMEM),
            pl.BlockSpec(memory_space=pltpu.VMEM),
        ],
        out_specs=pl.BlockSpec(memory_space=pl.ANY),
        scratch_shapes=[
            pltpu.VMEM((6, ROWS, K), jnp.bfloat16),
            pltpu.VMEM((10, ROWS, ROWS), jnp.float32),
            pltpu.VMEM((16, ROWS, ROWS), jnp.bfloat16),
            pltpu.SemaphoreType.DMA((NC,)),
            pltpu.SemaphoreType.DMA((5, NC)),
            pltpu.SemaphoreType.DMA((5, NC)),
            pltpu.SemaphoreType.DMA((16,)),
            pltpu.SemaphoreType.DMA((8, 2)),
        ],
        compiler_params=pltpu.CompilerParams(has_side_effects=True, vmem_limit_bytes=40 * 2**20),
        name="meet",
    )(panel, sizes, signs)


def place_kernel(blocks, front, tiles, out):
    group = lax.axis_index("group")
    member = lax.axis_index("member")
    half = pl.program_id(0)
    out[...] = front[...]
    run = 2 * group + half
    for g in range(8):
        for i in range(2):
            r = blocks[g, 2 * member + i] - SIDE * member
            for j in range(2):
                c = blocks[g, 2 * run + j] - SIDE * run
                where = (pl.ds(pl.multiple_of(r * B, B), B), pl.ds(pl.multiple_of(c * B, B), B))
                out[where] -= tiles[g, 0, i * B:(i + 1) * B, j * B:(j + 1) * B].astype(jnp.float32)


def place(blocks, front, tiles):
    return pl.pallas_call(
        place_kernel,
        grid=(2,),
        out_shape=jax.ShapeDtypeStruct(front.shape, jnp.float32),
        in_specs=[
            pl.BlockSpec(memory_space=pltpu.SMEM),
            pl.BlockSpec((512, 512), lambda h: (0, h)),
            pl.BlockSpec((8, 1, ROWS, ROWS), lambda h: (0, h, 0, 0)),
        ],
        out_specs=pl.BlockSpec((512, 512), lambda h: (0, h)),
        compiler_params=pltpu.CompilerParams(vmem_limit_bytes=32 * 2**20),
        name="place",
    )(blocks, front, tiles)


def local(root_front, child_panels, pivot_sizes, pivot_signs, child_blocks):
    tiles = meet(child_panels, pivot_sizes, pivot_signs)
    return place(child_blocks, root_front, tiles)


def solution(mesh):
    placed = (
        P("member", "group"),
        P("group", "member", None),
        P("group", None),
        P("group", None),
        P(),
    )
    return jax.shard_map(
        local, mesh=mesh, in_specs=placed, out_specs=P("member", "group"), check_vma=False
    )
```

time: 378 us -> 131 us (0.35)
  the two profiles are of different devices: /device:TPU:7 before, /device:TPU:5 now
where the time goes in v1:
time: 131 us; the launch traced here: 130 us
  Pallas kernels  127 us (97%)
  local copies, waits for them, and re-layouts  3.03 us (2%)
    pallas_call x1, Pallas kernels, meet(): pl.pallas_call(meet_kernel, out_shape=jax.ShapeDtypeStruct((8, 2, ROWS, R...  125 us
    unnamed x10, local copies, waits for them, and re-layouts  3.03 us
    pallas_call x1, Pallas kernels, place(): pl.pallas_call(place_kernel, grid=(2,), out_shape=jax.ShapeDtypeStruct(fr...  2.74 us

profile of v1, /device:TPU:5, one launch (start us, length us, event | category | flops | bytes accessed | tf_op | source)
XLA Modules:
  0.0 130.4 jit_solution(4530595693518544826)
XLA Ops:
  0.0 0.0 copy-start
  0.0 1.6 %copy-done = bf16[1,256,4096]{2,1,0:T(8,128)(2,1)S(1)} copy-done((bf16[1,256,4096]{2,1,0:T(8,128)(2,1)S(1)}, bf16[1,256,4096]{2,1,0:T(8,128)(2,1)}, u32[]{:S(2)}) %copy-start) | copy-done | bytes 2097176
  1.6 0.0 copy-start.2
  1.6 0.7 copy-done.2
  2.3 0.0 copy-start.3
  2.3 0.7 copy-done.3
  3.0 0.0 copy-start.1
  3.0 0.0 copy-start.4
  3.0 124.6 %meet.1.tiles = bf16[8,2,256,256]{3,2,1,0:T(8,128)(2,1)S(1)} custom-call(bf16[1,256,4096]{2,1,0:T(8,128)(2,1)S(1)} %copy-done, f32[1,4096]{1,0:T(1,128)S(1)} %copy-done.2, s32[1,4096]{1,0:T(1,128)S(1)} %copy-done.3), custom_call_target="tpu_custom_call" | custom-call | tf_op jit(solution)/shard_map/meet/pallas_call | solution.py:205
  127.6 0.0 copy-done.1
  127.6 0.0 copy-done.4
  127.7 2.7 %place.1 = f32[512,1024]{1,0:T(8,128)} custom-call(s32[8,32]{1,0:T(8,128)S(1)} %copy-done.4, f32[512,1024]{1,0:T(8,128)S(1)} %copy-done.1, bf16[8,2,256,256]{3,2,1,0:T(8,128)(2,1)S(1)} %meet.1.tiles), custom_call_target="tpu_custom_call" | custom-call | tf_op jit(solution)/shard_map/place/pallas_call | solution.py:245
Async XLA Ops:
  0.0 1.6 %copy-start = (bf16[1,256,4096]{2,1,0:T(8,128)(2,1)S(1)}, bf16[1,256,4096]{2,1,0:T(8,128)(2,1)}, u32[]{:S(2)}) copy-start(bf16[1,256,4096]{2,1,0:T(8,128)(2,1)} %panel.1) | copy-start | bytes 6291460
  1.6 0.7 copy-start.2
  2.3 0.7 copy-start.3
  3.0 124.6 %copy-start.1 = (f32[512,1024]{1,0:T(8,128)S(1)}, f32[512,1024]{1,0:T(8,128)}, u32[]{:S(2)}) copy-start(f32[512,1024]{1,0:T(8,128)} %front.1) | copy-start | bytes 6291460
  3.0 124.6 %copy-start.4 = (s32[8,32]{1,0:T(8,128)S(1)}, s32[8,32]{1,0:T(8,128)}, u32[]{:S(2)}) copy-start(s32[8,32]{1,0:T(8,128)} %blocks.1) | copy-start | bytes 3076

commit v2 on v1

v2 whole, which is shorter than its diff:
```python
import jax
import jax.numpy as jnp
from jax import lax
from jax.experimental import pallas as pl
from jax.experimental.pallas import tpu as pltpu
from jax.sharding import PartitionSpec as P

B = 128
ROWS = 256
K = 4096
NC = 8
KC = K // NC
AHEAD = 3
SIDE = 4
pivot_floor = 0.1

TRI = ((0, 0), (0, 1), (1, 0), (1, 1), (0, 2), (2, 0))
PAIRS = (
    (0, 0, False),
    (0, 1, True),
    (0, 2, True),
    (2, 1, True),
    (0, 3, True),
    (0, 4, False),
    (2, 4, True),
    (0, 5, False),
    (5, 1, True),
    (5, 4, False),
)

TILES = tuple((n, a, b, False) for n, (a, b, _) in enumerate(PAIRS)) + tuple(
    (n, b, a, True) for n, (a, b, both) in enumerate(PAIRS) if both
)
NEAR, CORNER, FAR = (0, 1, 2, 3), (4,), (5, 6, 7, 8, 9)
PASS_NEAR, PASS_FAR = 3, 2


def dot_nt(left, right):
    return lax.dot_general(left, right, (((1,), (1,)), ((), ())), preferred_element_type=jnp.float32)


def meet_kernel(
    panel, sizes_in, signs_in, arrived, pan, sizes, signs, acc, stage, mine,
    load_sem, row_sem, hop_send, hop_recv, relay_send, relay_recv, tile_send, tile_recv,
):
    group = lax.axis_index("group")
    member = lax.axis_index("member")
    row, col = member // SIDE, member % SIDE
    turn = 1 - 2 * (group % 2)

    def at(offset):
        y = (row + turn * offset[0] + SIDE) % SIDE
        z = (col + turn * offset[1] + SIDE) % SIDE
        return y * SIDE + z

    to_z, to_y = at((0, -1)), at((-1, 0))

    def cols(k):
        return pl.ds(pl.multiple_of(k * KC, KC), KC)

    def load(k):
        return pltpu.make_async_copy(panel.at[0, :, cols(k)], pan.at[0, :, cols(k)], load_sem.at[k])

    load_sizes = pltpu.make_async_copy(sizes_in, sizes, row_sem.at[0])
    load_signs = pltpu.make_async_copy(signs_in, signs, row_sem.at[1])
    load_sizes.start()
    for k in range(NC):
        load(k).start()
    load_signs.start()

    barrier = pltpu.get_barrier_semaphore()

    def greet(g, m):
        pl.semaphore_signal(
            barrier, inc=1, device_id={"group": g, "member": m}, device_id_type=pl.DeviceIdType.MESH
        )

    greet(group, at((0, 1)))
    greet(group, at((1, 0)))
    for offset in TRI[1:]:
        greet(group, at((-offset[0], -offset[1])))
    for step in range(1, 8):
        greet((group + step) % 8, member)
    greeted = 2 + len(TRI[1:]) + 7

    def hop(src, dst, k, target):
        return pltpu.make_async_remote_copy(
            src_ref=pan.at[src, :, cols(k)],
            dst_ref=pan.at[dst, :, cols(k)],
            send_sem=hop_send.at[dst - 1, k],
            recv_sem=hop_recv.at[dst - 1, k],
            device_id={"group": group, "member": target},
            device_id_type=pl.DeviceIdType.MESH,
        )

    def hops_own(k):
        return hop(0, 1, k, to_z), hop(0, 2, k, to_y)

    def hops_far(k):
        return hop(1, 4, k, to_z), hop(2, 5, k, to_y)

    def hops_corner(c):
        return hop(2, 3, 2 * c, to_z), hop(1, 3, 2 * c + 1, to_y)

    def start(pair):
        for copy in pair:
            copy.start()

    def landed(pair):
        for copy in pair:
            copy.wait_recv()

    load_sizes.wait()
    root = jnp.sqrt(jnp.maximum(sizes[...], pivot_floor))
    for k in range(NC):
        load(k).wait()
        s = slice(k * KC, (k + 1) * KC)
        pan[0, :, s] = (pan[0, :, s].astype(jnp.float32) * root[:, s]).astype(jnp.bfloat16)
        if k == 0:
            pl.semaphore_wait(barrier, greeted)
        if k < AHEAD:
            start(hops_own(k))
    load_signs.wait()

    def signed(slot, k):
        s = (2 * signs[:, cols(k)] - 1).astype(jnp.float32).astype(jnp.bfloat16)
        return pan[slot, :, cols(k)] * s

    def accumulate(n, left, right, k):
        prod = dot_nt(left, pan[right, :, cols(k)])

        @pl.when(k == 0)
        def _():
            acc[n] = prod

        @pl.when(k > 0)
        def _():
            acc[n] += prod

    def relay(slot, r):
        return pltpu.make_async_remote_copy(
            src_ref=stage.at[slot],
            dst_ref=mine.at[slot],
            send_sem=relay_send.at[slot],
            recv_sem=relay_recv.at[slot],
            device_id={"group": group, "member": at(TRI[r])},
            device_id_type=pl.DeviceIdType.MESH,
        )

    def column_of(r, c):
        return at((TRI[c][0] - TRI[r][0], TRI[c][1] - TRI[r][1]))

    def deliver(slot, r, c):
        column = column_of(r, c)
        owner, half = column // 2, column % 2

        @pl.when(owner == group)
        def _():
            pltpu.make_async_copy(mine.at[slot], arrived.at[group, half], tile_recv.at[group, half]).start()

        @pl.when(owner != group)
        def _():
            remote_tile(slot, owner, half).start()

    def remote_tile(slot, owner, half):
        return pltpu.make_async_remote_copy(
            src_ref=mine.at[slot],
            dst_ref=arrived.at[group, half],
            send_sem=tile_send.at[slot],
            recv_sem=tile_recv.at[group, half],
            device_id={"group": owner, "member": member},
            device_id_type=pl.DeviceIdType.MESH,
        )

    def ship(pairs):
        for here in (False, True):
            for slot, (n, r, c, flipped) in enumerate(TILES):
                if n not in pairs or here != (r == 0):
                    continue
                value = acc[n].astype(jnp.bfloat16)
                value = value.T if flipped else value
                if here:
                    mine[slot] = value
                    deliver(slot, r, c)
                else:
                    stage[slot] = value
                    relay(slot, r).start()

    def pass_on(pairs):
        for slot, (n, r, c, _) in enumerate(TILES):
            if n in pairs and r != 0:
                relay(slot, r).wait_recv()
                deliver(slot, r, c)

    def near(k, carry):
        own = signed(0, k)
        accumulate(0, own, 0, k)
        landed(hops_own(k))

        @pl.when(k + AHEAD < NC)
        def _():
            start(hops_own(k + AHEAD))

        @pl.when(k + AHEAD >= NC)
        def _():
            start(hops_far(k + AHEAD - NC))

        accumulate(1, own, 1, k)
        accumulate(2, own, 2, k)
        accumulate(3, signed(2, k), 1, k)
        return carry

    lax.fori_loop(0, NC, near, 0)
    ship(NEAR)

    def far(k, carry):
        landed(hops_far(k))

        @pl.when(k + AHEAD < NC)
        def _():
            start(hops_far(k + AHEAD))

        @pl.when(k + AHEAD >= NC)
        def _():
            start(hops_corner(k + AHEAD - NC))

        @pl.when(k == PASS_NEAR)
        def _():
            pass_on(NEAR)

        own = signed(0, k)
        accumulate(5, own, 4, k)
        accumulate(6, signed(2, k), 4, k)
        accumulate(7, own, 5, k)
        last = signed(5, k)
        accumulate(8, last, 1, k)
        accumulate(9, last, 4, k)
        return carry

    lax.fori_loop(0, NC, far, 0)
    for c in range(AHEAD, NC // 2):
        start(hops_corner(c))
    ship(FAR)

    def corner(c, carry):
        landed(hops_corner(c))

        @pl.when(c == PASS_FAR)
        def _():
            pass_on(FAR)

        accumulate(4, signed(0, 2 * c), 3, 2 * c)
        accumulate(4, signed(0, 2 * c + 1), 3, 2 * c + 1)
        return carry

    lax.fori_loop(0, NC // 2, corner, 0)
    ship(CORNER)
    pass_on(CORNER)

    def drain(k, carry):
        for copy in hops_own(k) + hops_far(k):
            copy.wait_send()
        hop(2, 3, k, to_z).wait_send()
        return carry

    lax.fori_loop(0, NC, drain, 0)
    for slot, (_, r, c, _) in enumerate(TILES):
        if r != 0:
            relay(slot, r).wait_send()
        column = column_of(r, c)

        @pl.when(column // 2 != group)
        def _():
            remote_tile(slot, column // 2, column % 2).wait_send()

    for g in range(8):
        for j in range(2):
            pltpu.make_async_copy(stage.at[0], arrived.at[g, j], tile_recv.at[g, j]).wait()


def meet(panel, sizes, signs):
    return pl.pallas_call(
        meet_kernel,
        out_shape=jax.ShapeDtypeStruct((8, 2, ROWS, ROWS), jnp.bfloat16),
        in_specs=[pl.BlockSpec(memory_space=pltpu.HBM)] * 3,
        out_specs=pl.BlockSpec(memory_space=pl.ANY),
        scratch_shapes=[
            pltpu.VMEM((6, ROWS, K), jnp.bfloat16),
            pltpu.VMEM((1, K), jnp.float32),
            pltpu.VMEM((1, K), jnp.int32),
            pltpu.VMEM((10, ROWS, ROWS), jnp.float32),
            pltpu.VMEM((16, ROWS, ROWS), jnp.bfloat16),
            pltpu.VMEM((16, ROWS, ROWS), jnp.bfloat16),
            pltpu.SemaphoreType.DMA((NC,)),
            pltpu.SemaphoreType.DMA((2,)),
            pltpu.SemaphoreType.DMA((5, NC)),
            pltpu.SemaphoreType.DMA((5, NC)),
            pltpu.SemaphoreType.DMA((16,)),
            pltpu.SemaphoreType.DMA((16,)),
            pltpu.SemaphoreType.DMA((16,)),
            pltpu.SemaphoreType.DMA((8, 2)),
        ],
        compiler_params=pltpu.CompilerParams(
            collective_id=0, has_side_effects=True, vmem_limit_bytes=59 * 2**20
        ),
        name="meet",
    )(panel, sizes, signs)


def place_kernel(blocks, front, tiles, out):
    group = lax.axis_index("group")
    member = lax.axis_index("member")
    half = pl.program_id(0)
    out[...] = front[...]
    run = 2 * group + half
    for g in range(8):
        for i in range(2):
            r = blocks[g, 2 * member + i] - SIDE * member
            for j in range(2):
                c = blocks[g, 2 * run + j] - SIDE * run
                where = (pl.ds(pl.multiple_of(r * B, B), B), pl.ds(pl.multiple_of(c * B, B), B))
                out[where] -= tiles[g, 0, i * B:(i + 1) * B, j * B:(j + 1) * B].astype(jnp.float32)


def place(blocks, front, tiles):
    return pl.pallas_call(
        place_kernel,
        grid=(2,),
        out_shape=jax.ShapeDtypeStruct(front.shape, jnp.float32),
        in_specs=[
            pl.BlockSpec(memory_space=pltpu.SMEM),
            pl.BlockSpec((512, 512), lambda h: (0, h)),
            pl.BlockSpec((8, 1, ROWS, ROWS), lambda h: (0, h, 0, 0)),
        ],
        out_specs=pl.BlockSpec((512, 512), lambda h: (0, h)),
        compiler_params=pltpu.CompilerParams(vmem_limit_bytes=32 * 2**20),
        name="place",
    )(blocks, front, tiles)


def local(root_front, child_panels, pivot_sizes, pivot_signs, child_blocks):
    tiles = meet(child_panels, pivot_sizes, pivot_signs)
    return place(child_blocks, root_front, tiles)


def solution(mesh):
    placed = (
        P("member", "group"),
        P("group", "member", None),
        P("group", None),
        P("group", None),
        P(),
    )
    return jax.shard_map(
        local, mesh=mesh, in_specs=placed, out_specs=P("member", "group"), check_vma=False
    )
```

time: 131 us -> 94.6 us (0.72)
  the two profiles are of different devices: /device:TPU:5 before, /device:TPU:7 now
where the time goes in v2:
time: 94.6 us; the launch traced here: 94.5 us
  Pallas kernels  92.8 us (98%)
  local copies, waits for them, and re-layouts  1.59 us (2%)
    pallas_call x1, Pallas kernels, meet(): pl.pallas_call(meet_kernel, out_shape=jax.ShapeDtypeStruct((8, 2, ROWS, R...  90.1 us
    pallas_call x1, Pallas kernels, place(): pl.pallas_call(place_kernel, grid=(2,), out_shape=jax.ShapeDtypeStruct(fr...  2.71 us

profile of v2, /device:TPU:7, one launch (start us, length us, event | category | flops | bytes accessed | tf_op | source)
XLA Modules:
  0.0 94.5 jit_solution(5846680867293797481)
XLA Ops:
  0.0 0.0 copy-start.2
  0.0 0.0 copy-start.1
  0.0 90.1 %meet.1.tiles = bf16[8,2,256,256]{3,2,1,0:T(8,128)(2,1)} custom-call(bf16[1,256,4096]{2,1,0:T(8,128)(2,1)} %panel.1, f32[1,4096]{1,0:T(1,128)} %sizes_in.1, s32[1,4096]{1,0:T(1,128)} %signs_in.1), custom_call_target="tpu_custom_call" | custom-call | tf_op jit(solution)/shard_map/meet/pallas_call | solution.py:282
  90.1 0.0 copy-done.2
  90.1 0.0 copy-done.1
  90.2 0.0 copy-start
  90.2 1.6 %copy-done = bf16[8,2,256,256]{3,2,1,0:T(8,128)(2,1)S(1)} copy-done((bf16[8,2,256,256]{3,2,1,0:T(8,128)(2,1)S(1)}, bf16[8,2,256,256]{3,2,1,0:T(8,128)(2,1)}, u32[]{:S(2)}) %copy-start) | copy-done | bytes 2097176
  91.7 2.7 %place.1 = f32[512,1024]{1,0:T(8,128)} custom-call(s32[8,32]{1,0:T(8,128)S(1)} %copy-done.2, f32[512,1024]{1,0:T(8,128)S(1)} %copy-done.1, bf16[8,2,256,256]{3,2,1,0:T(8,128)(2,1)S(1)} %copy-done), custom_call_target="tpu_custom_call" | custom-call | tf_op jit(solution)/shard_map/place/pallas_call | solution.py:326
Async XLA Ops:
  0.0 90.1 %copy-start.2 = (s32[8,32]{1,0:T(8,128)S(1)}, s32[8,32]{1,0:T(8,128)}, u32[]{:S(2)}) copy-start(s32[8,32]{1,0:T(8,128)} %blocks.1) | copy-start | bytes 3076
  0.0 90.1 %copy-start.1 = (f32[512,1024]{1,0:T(8,128)S(1)}, f32[512,1024]{1,0:T(8,128)}, u32[]{:S(2)}) copy-start(f32[512,1024]{1,0:T(8,128)} %front.1) | copy-start | bytes 6291460
  90.2 1.6 %copy-start = (bf16[8,2,256,256]{3,2,1,0:T(8,128)(2,1)S(1)}, bf16[8,2,256,256]{3,2,1,0:T(8,128)(2,1)}, u32[]{:S(2)}) copy-start(bf16[8,2,256,256]{3,2,1,0:T(8,128)(2,1)} %meet.1.tiles) | copy-start | bytes 6291460

commit v3 on v2

v3 whole, which is shorter than its diff:
```python
import jax
import jax.numpy as jnp
from jax import lax
from jax.experimental import pallas as pl
from jax.experimental.pallas import tpu as pltpu
from jax.sharding import PartitionSpec as P

B = 128
ROWS = 256
K = 4096
NC = 8
KC = K // NC
KH = 2 * KC
AHEAD = 3
SIDE = 4
pivot_floor = 0.1

CROSS = ((0, 0), (0, 1), (1, 0), (0, 3), (0, 2), (2, 0))
PAIRS = (
    (0, 0), (0, 1), (0, 2), (2, 1),
    (0, 3), (2, 3), (5, 3),
    (0, 4), (2, 4), (0, 5), (1, 5),
    (4, 5),
)
TILES = tuple((n, a, b, False) for n, (a, b) in enumerate(PAIRS) if n != 6) + tuple(
    (n, PAIRS[n][1], PAIRS[n][0], True) for n in (2, 3, 5, 6, 8)
)
NEAR, CORNER, FAR, LAST = (0, 1, 2, 3), (4, 5, 6), (7, 8, 9, 10), (11,)
WHOLE = 2
PASS_NEAR, PASS_FAR, PASS_LAST = 2, 2, 2


def dot_nt(left, right):
    return lax.dot_general(left, right, (((1,), (1,)), ((), ())), preferred_element_type=jnp.float32)


def half_rows(h):
    return pl.ds(h * B if isinstance(h, int) else pl.multiple_of(h * B, B), B)


def part(ref, flipped, h):
    if h == WHOLE:
        return ref
    return ref.at[half_rows(h), :] if flipped else ref.at[:, half_rows(h)]


def meet_kernel(
    panel, sizes_in, signs_in, arrived, pan, sizes, signs, acc, stage, mine,
    load_sem, row_sem, hop_send, hop_recv, relay_send, relay_recv, tile_send, tile_recv,
):
    group = lax.axis_index("group")
    member = lax.axis_index("member")
    row, col = member // SIDE, member % SIDE
    odd = group % 2

    def at(offset):
        across, along = offset
        y = (row + jnp.where(odd == 0, across, -along) + SIDE) % SIDE
        z = (col + jnp.where(odd == 0, along, -across) + SIDE) % SIDE
        return y * SIDE + z

    to_back, to_across, to_ahead = at((0, -1)), at((-1, 0)), at((0, 1))

    def cols(k):
        return pl.ds(pl.multiple_of(k * KC, KC), KC)

    def load(k):
        return pltpu.make_async_copy(panel.at[0, :, cols(k)], pan.at[0, :, cols(k)], load_sem.at[k])

    load_sizes = pltpu.make_async_copy(sizes_in, sizes, row_sem.at[0])
    load_signs = pltpu.make_async_copy(signs_in, signs, row_sem.at[1])
    load_sizes.start()
    for k in range(NC):
        load(k).start()
    load_signs.start()

    barrier = pltpu.get_barrier_semaphore()

    def greet(g, m):
        pl.semaphore_signal(
            barrier, inc=1, device_id={"group": g, "member": m}, device_id_type=pl.DeviceIdType.MESH
        )

    for offset in ((0, 1), (1, 0), (0, -1)):
        greet(group, at(offset))
    rows_of = sorted({r for _, r, _, _ in TILES if r != 0})
    for r in rows_of:
        greet(group, at((-CROSS[r][0], -CROSS[r][1])))
    for step in range(1, 8):
        greet((group + step) % 8, member)
    greeted = 3 + len(rows_of) + 7

    def hop(src, dst, rows, columns, n, target):
        return pltpu.make_async_remote_copy(
            src_ref=pan.at[src, rows, columns],
            dst_ref=pan.at[dst, rows, columns],
            send_sem=hop_send.at[dst - 1, n],
            recv_sem=hop_recv.at[dst - 1, n],
            device_id={"group": group, "member": target},
            device_id_type=pl.DeviceIdType.MESH,
        )

    def wide(kk):
        return pl.ds(pl.multiple_of(kk * KH, KH), KH)

    def hops_own(k):
        return hop(0, 1, slice(None), cols(k), k, to_back), hop(0, 2, slice(None), cols(k), k, to_across)

    def hops_far(f):
        rows, columns = half_rows(f // 4), wide(f % 4)
        return hop(1, 4, rows, columns, f, to_back), hop(2, 5, rows, columns, f, to_across)

    def hops_corner(c):
        h, i = c // 2, c % 2
        return (
            hop(4, 3, half_rows(h), wide(i), 4 * h + i, to_back),
            hop(0, 3, half_rows(h), wide(2 + i), 4 * h + 2 + i, to_ahead),
        )

    def start(pair):
        for copy in pair:
            copy.start()

    def landed(pair):
        for copy in pair:
            copy.wait_recv()

    load_sizes.wait()
    root = jnp.sqrt(jnp.maximum(sizes[...], pivot_floor))
    for k in range(NC):
        load(k).wait()
        s = slice(k * KC, (k + 1) * KC)
        pan[0, :, s] = (pan[0, :, s].astype(jnp.float32) * root[:, s]).astype(jnp.bfloat16)
        if k == 0:
            pl.semaphore_wait(barrier, greeted)
        if k < AHEAD:
            start(hops_own(k))
    load_signs.wait()

    def signed(slot, rows, columns):
        s = (2 * signs[:, columns] - 1).astype(jnp.float32).astype(jnp.bfloat16)
        return pan[slot, rows, columns] * s

    def accumulate(n, rows, columns, prod, first):
        @pl.when(first)
        def _():
            acc[n, rows, columns] = prod

        @pl.when(jnp.logical_not(first))
        def _():
            acc[n, rows, columns] += prod

    def relay(slot, h):
        _, r, _, flipped = TILES[slot]
        return pltpu.make_async_remote_copy(
            src_ref=part(stage.at[slot], flipped, h),
            dst_ref=part(mine.at[slot], flipped, h),
            send_sem=relay_send.at[slot, h % 2],
            recv_sem=relay_recv.at[slot, h % 2],
            device_id={"group": group, "member": at(CROSS[r])},
            device_id_type=pl.DeviceIdType.MESH,
        )

    def home(slot):
        _, r, c, _ = TILES[slot]
        column = at((CROSS[c][0] - CROSS[r][0], CROSS[c][1] - CROSS[r][1]))
        return column // 2, column % 2

    def to_owner(slot, h):
        owner, side = home(slot)
        flipped = TILES[slot][3]
        return pltpu.make_async_remote_copy(
            src_ref=part(mine.at[slot], flipped, h),
            dst_ref=part(arrived.at[group, side], flipped, h),
            send_sem=tile_send.at[slot, h % 2],
            recv_sem=tile_recv.at[group, side],
            device_id={"group": owner, "member": member},
            device_id_type=pl.DeviceIdType.MESH,
        )

    def deliver(slot, h):
        owner, side = home(slot)
        flipped = TILES[slot][3]

        @pl.when(owner == group)
        def _():
            pltpu.make_async_copy(
                part(mine.at[slot], flipped, h),
                part(arrived.at[group, side], flipped, h),
                tile_recv.at[group, side],
            ).start()

        @pl.when(owner != group)
        def _():
            to_owner(slot, h).start()

    def ship(products, h):
        for here in (False, True):
            for slot, (n, r, _, flipped) in enumerate(TILES):
                if n not in products or here != (r == 0):
                    continue
                value = (acc[n] if h == WHOLE else acc[n, :, half_rows(h)]).astype(jnp.bfloat16)
                part((mine if here else stage).at[slot], flipped, h)[...] = value.T if flipped else value
                if here:
                    deliver(slot, h)
                else:
                    relay(slot, h).start()

    def pass_on(products, h):
        for slot, (n, r, _, _) in enumerate(TILES):
            if n in products and r != 0:
                relay(slot, h).wait_recv()
                deliver(slot, h)

    everything = slice(None)

    def near(k, carry):
        first = k == 0
        own = signed(0, everything, cols(k))
        accumulate(0, everything, everything, dot_nt(own, pan[0, :, cols(k)]), first)
        landed(hops_own(k))

        @pl.when(k + AHEAD < NC)
        def _():
            start(hops_own(k + AHEAD))

        @pl.when(k + AHEAD >= NC)
        def _():
            start(hops_far(k + AHEAD - NC))

        accumulate(1, everything, everything, dot_nt(own, pan[1, :, cols(k)]), first)
        accumulate(2, everything, everything, dot_nt(own, pan[2, :, cols(k)]), first)
        accumulate(3, everything, everything, dot_nt(signed(2, everything, cols(k)), pan[1, :, cols(k)]), first)
        return carry

    lax.fori_loop(0, NC, near, 0)
    ship(NEAR, WHOLE)

    def far(h, kk):
        f = 4 * h + kk
        landed(hops_far(f))

        @pl.when(f + AHEAD < NC)
        def _():
            start(hops_far(f + AHEAD))

        @pl.when(f + AHEAD >= NC)
        def _():
            start(hops_corner(f + AHEAD - NC))

        first = kk == 0
        here, where = half_rows(h), wide(kk)
        along = signed(4, here, where)
        accumulate(7, everything, here, dot_nt(pan[0, :, where], along), first)
        accumulate(8, everything, here, dot_nt(pan[2, :, where], along), first)
        across = signed(5, here, where)
        accumulate(9, everything, here, dot_nt(pan[0, :, where], across), first)
        accumulate(10, everything, here, dot_nt(pan[1, :, where], across), first)
        if h == 0:
            accumulate(11, here, here, dot_nt(pan[4, here, where], across), first)
        else:
            accumulate(11, everything, here, dot_nt(pan[4, :, where], across), first)
            accumulate(11, here, half_rows(0), dot_nt(along, pan[5, half_rows(0), where]), first)

    def far_first(kk, carry):
        far(0, kk)

        @pl.when(kk == PASS_NEAR)
        def _():
            pass_on(NEAR, WHOLE)

        return carry

    lax.fori_loop(0, 4, far_first, 0)
    ship(FAR, 0)

    def far_second(kk, carry):
        far(1, kk)

        @pl.when(kk == PASS_FAR)
        def _():
            pass_on(FAR, 0)

        return carry

    lax.fori_loop(0, 4, far_second, 0)
    for c in range(AHEAD, 4):
        start(hops_corner(c))
    ship(FAR, 1)
    ship(LAST, WHOLE)

    def corner(h, i):
        landed(hops_corner(2 * h + i))
        here = half_rows(h)
        low, high = signed(3, here, wide(i)), signed(3, here, wide(2 + i))
        for n in CORNER:
            left = PAIRS[n][0]
            prod = dot_nt(pan[left, :, wide(i)], low)
            prod += dot_nt(pan[left, :, wide(2 + i)], high)
            accumulate(n, everything, here, prod, i == 0)

    for h in range(2):
        for i in range(2):
            corner(h, i)
            if 2 * h + i == PASS_LAST:
                pass_on(FAR, 1)
                pass_on(LAST, WHOLE)
        ship(CORNER, h)
    pass_on(CORNER, 0)
    pass_on(CORNER, 1)

    def drain(k, carry):
        for copy in hops_own(k) + hops_far(k):
            copy.wait_send()
        return carry

    lax.fori_loop(0, NC, drain, 0)
    for c in range(4):
        for copy in hops_corner(c):
            copy.wait_send()
    for slot, (n, r, _, _) in enumerate(TILES):
        for h in (WHOLE,) if n in NEAR + LAST else (0, 1):
            if r != 0:
                relay(slot, h).wait_send()

            @pl.when(home(slot)[0] != group)
            def _():
                to_owner(slot, h).wait_send()

    for g in range(8):
        for j in range(2):
            pltpu.make_async_copy(mine.at[0], arrived.at[g, j], tile_recv.at[g, j]).wait()


def meet(panel, sizes, signs):
    return pl.pallas_call(
        meet_kernel,
        out_shape=jax.ShapeDtypeStruct((8, 2, ROWS, ROWS), jnp.bfloat16),
        in_specs=[pl.BlockSpec(memory_space=pltpu.HBM)] * 3,
        out_specs=pl.BlockSpec(memory_space=pl.ANY),
        scratch_shapes=[
            pltpu.VMEM((6, ROWS, K), jnp.bfloat16),
            pltpu.VMEM((1, K), jnp.float32),
            pltpu.VMEM((1, K), jnp.int32),
            pltpu.VMEM((12, ROWS, ROWS), jnp.float32),
            pltpu.VMEM((16, ROWS, ROWS), jnp.bfloat16),
            pltpu.VMEM((16, ROWS, ROWS), jnp.bfloat16),
            pltpu.SemaphoreType.DMA((NC,)),
            pltpu.SemaphoreType.DMA((2,)),
            pltpu.SemaphoreType.DMA((5, NC)),
            pltpu.SemaphoreType.DMA((5, NC)),
            pltpu.SemaphoreType.DMA((16, 2)),
            pltpu.SemaphoreType.DMA((16, 2)),
            pltpu.SemaphoreType.DMA((16, 2)),
            pltpu.SemaphoreType.DMA((8, 2)),
        ],
        compiler_params=pltpu.CompilerParams(
            collective_id=0, has_side_effects=True, vmem_limit_bytes=59 * 2**20
        ),
        name="meet",
    )(panel, sizes, signs)


def place_kernel(blocks_in, front, tiles_in, out, blocks, total, tiles, blocks_sem, front_sem, tiles_sem, out_sem):
    group = lax.axis_index("group")
    member = lax.axis_index("member")
    width = 4 * B

    def load_front(j):
        return pltpu.make_async_copy(
            front.at[:, j * width:(j + 1) * width], total.at[:, j * width:(j + 1) * width], front_sem.at[j]
        )

    def load_tile(g, j):
        return pltpu.make_async_copy(tiles_in.at[g, j], tiles.at[g, j], tiles_sem.at[g, j])

    def store(j):
        return pltpu.make_async_copy(
            total.at[:, j * width:(j + 1) * width], out.at[:, j * width:(j + 1) * width], out_sem.at[j]
        )

    load_blocks = pltpu.make_async_copy(blocks_in, blocks, blocks_sem)
    load_blocks.start()
    for j in range(2):
        load_front(j).start()
        for g in range(8):
            load_tile(g, j).start()
    load_blocks.wait()
    for j in range(2):
        run = 2 * group + j
        load_front(j).wait()
        for g in range(8):
            load_tile(g, j).wait()
            for a in range(2):
                r = blocks[g, 2 * member + a] - SIDE * member
                for b in range(2):
                    c = blocks[g, 2 * run + b] - SIDE * run + SIDE * j
                    where = (pl.ds(pl.multiple_of(r * B, B), B), pl.ds(pl.multiple_of(c * B, B), B))
                    total[where] -= tiles[g, j, a * B:(a + 1) * B, b * B:(b + 1) * B].astype(jnp.float32)
        store(j).start()
    for j in range(2):
        store(j).wait()


def place(blocks, front, tiles):
    return pl.pallas_call(
        place_kernel,
        out_shape=jax.ShapeDtypeStruct(front.shape, jnp.float32),
        in_specs=[pl.BlockSpec(memory_space=pl.ANY)] * 3,
        out_specs=pl.BlockSpec(memory_space=pl.ANY),
        scratch_shapes=[
            pltpu.SMEM(blocks.shape, jnp.int32),
            pltpu.VMEM(front.shape, jnp.float32),
            pltpu.VMEM(tiles.shape, jnp.bfloat16),
            pltpu.SemaphoreType.DMA,
            pltpu.SemaphoreType.DMA((2,)),
            pltpu.SemaphoreType.DMA((8, 2)),
            pltpu.SemaphoreType.DMA((2,)),
        ],
        compiler_params=pltpu.CompilerParams(vmem_limit_bytes=62 * 2**20),
        name="place",
    )(blocks, front, tiles)


def local(root_front, child_panels, pivot_sizes, pivot_signs, child_blocks):
    tiles = meet(child_panels, pivot_sizes, pivot_signs)
    return place(child_blocks, root_front, tiles)


def solution(mesh):
    placed = (
        P("member", "group"),
        P("group", "member", None),
        P("group", None),
        P("group", None),
        P(),
    )
    return jax.shard_map(
        local, mesh=mesh, in_specs=placed, out_specs=P("member", "group"), check_vma=False
    )
```

time: 94.6 us -> 89.4 us (0.945)
  Pallas kernels: 92.8 us -> 89.1 us
  local copies, waits for them, and re-layouts: 1.59 us -> 0 us
    pallas_call x1, Pallas kernels: 90.1 us -> 85.2 us  [meet(): pl.pallas_call(meet_kernel, out_shape=jax.ShapeDtypeStruct((8, 2, ROWS, R...]
    unnamed x6 -> x0, local copies, waits for them, and re-layouts: 1.59 us -> none
    pallas_call x1, Pallas kernels: 2.71 us -> 3.88 us  [place(): pl.pallas_call(place_kernel, out_shape=jax.ShapeDtypeStruct(front.shape,...]
where the time goes in v3:
time: 89.4 us; the launch traced here: 89.1 us
  Pallas kernels  89.1 us (100%)
    pallas_call x1, Pallas kernels, meet(): pl.pallas_call(meet_kernel, out_shape=jax.ShapeDtypeStruct((8, 2, ROWS, R...  85.2 us
    pallas_call x1, Pallas kernels, place(): pl.pallas_call(place_kernel, out_shape=jax.ShapeDtypeStruct(front.shape,...  3.88 us

profile of v3, /device:TPU:7, one launch (start us, length us, event | category | flops | bytes accessed | tf_op | source)
XLA Modules:
  0.0 89.1 jit_solution(3499086168942473290)
XLA Ops:
  0.0 85.2 %meet.1.tiles_in = bf16[8,2,256,256]{3,2,1,0:T(8,128)(2,1)} custom-call(bf16[1,256,4096]{2,1,0:T(8,128)(2,1)} %panel.1, f32[1,4096]{1,0:T(1,128)} %sizes_in.1, s32[1,4096]{1,0:T(1,128)} %signs_in.1), custom_call_target="tpu_custom_call" | custom-call | tf_op jit(solution)/shard_map/meet/pallas_call | solution.py:336
  85.2 3.9 %place.1 = f32[512,1024]{1,0:T(8,128)} custom-call(s32[8,32]{1,0:T(8,128)} %blocks_in.1, f32[512,1024]{1,0:T(8,128)} %front.1, bf16[8,2,256,256]{3,2,1,0:T(8,128)(2,1)} %meet.1.tiles_in), custom_call_target="tpu_custom_call" | custom-call | tf_op jit(solution)/shard_map/place/pallas_call | solution.py:406

commit v4 on v3

--- a/solution.py
+++ b/solution.py
@@ -27,7 +27,8 @@
 )
 NEAR, CORNER, FAR, LAST = (0, 1, 2, 3), (4, 5, 6), (7, 8, 9, 10), (11,)
 WHOLE = 2
-PASS_NEAR, PASS_FAR, PASS_LAST = 2, 2, 2
+PASS_NEAR, PASS_FAR = 2, 2
+EARLY = 2
 
 
 def dot_nt(left, right):
@@ -136,19 +137,14 @@
         if k < AHEAD:
             start(hops_own(k))
     load_signs.wait()
+    acc[...] = jnp.zeros_like(acc)
 
     def signed(slot, rows, columns):
         s = (2 * signs[:, columns] - 1).astype(jnp.float32).astype(jnp.bfloat16)
         return pan[slot, rows, columns] * s
 
-    def accumulate(n, rows, columns, prod, first):
-        @pl.when(first)
-        def _():
-            acc[n, rows, columns] = prod
-
-        @pl.when(jnp.logical_not(first))
-        def _():
-            acc[n, rows, columns] += prod
+    def accumulate(n, rows, columns, prod):
+        acc[n, rows, columns] += prod
 
     def relay(slot, h):
         _, r, _, flipped = TILES[slot]
@@ -215,9 +211,8 @@
     everything = slice(None)
 
     def near(k, carry):
-        first = k == 0
         own = signed(0, everything, cols(k))
-        accumulate(0, everything, everything, dot_nt(own, pan[0, :, cols(k)]), first)
+        accumulate(0, everything, everything, dot_nt(own, pan[0, :, cols(k)]))
         landed(hops_own(k))
 
         @pl.when(k + AHEAD < NC)
@@ -228,9 +223,9 @@
         def _():
             start(hops_far(k + AHEAD - NC))
 
-        accumulate(1, everything, everything, dot_nt(own, pan[1, :, cols(k)]), first)
-        accumulate(2, everything, everything, dot_nt(own, pan[2, :, cols(k)]), first)
-        accumulate(3, everything, everything, dot_nt(signed(2, everything, cols(k)), pan[1, :, cols(k)]), first)
+        accumulate(1, everything, everything, dot_nt(own, pan[1, :, cols(k)]))
+        accumulate(2, everything, everything, dot_nt(own, pan[2, :, cols(k)]))
+        accumulate(3, everything, everything, dot_nt(signed(2, everything, cols(k)), pan[1, :, cols(k)]))
         return carry
 
     lax.fori_loop(0, NC, near, 0)
@@ -244,23 +239,22 @@
         def _():
             start(hops_far(f + AHEAD))
 
-        @pl.when(f + AHEAD >= NC)
+        @pl.when(jnp.logical_and(f + AHEAD >= NC, f + AHEAD < NC + EARLY))
         def _():
             start(hops_corner(f + AHEAD - NC))
 
-        first = kk == 0
         here, where = half_rows(h), wide(kk)
         along = signed(4, here, where)
-        accumulate(7, everything, here, dot_nt(pan[0, :, where], along), first)
-        accumulate(8, everything, here, dot_nt(pan[2, :, where], along), first)
+        accumulate(7, everything, here, dot_nt(pan[0, :, where], along))
+        accumulate(8, everything, here, dot_nt(pan[2, :, where], along))
         across = signed(5, here, where)
-        accumulate(9, everything, here, dot_nt(pan[0, :, where], across), first)
-        accumulate(10, everything, here, dot_nt(pan[1, :, where], across), first)
+        accumulate(9, everything, here, dot_nt(pan[0, :, where], across))
+        accumulate(10, everything, here, dot_nt(pan[1, :, where], across))
         if h == 0:
-            accumulate(11, here, here, dot_nt(pan[4, here, where], across), first)
+            accumulate(11, here, here, dot_nt(pan[4, here, where], across))
         else:
-            accumulate(11, everything, here, dot_nt(pan[4, :, where], across), first)
-            accumulate(11, here, half_rows(0), dot_nt(along, pan[5, half_rows(0), where]), first)
+            accumulate(11, everything, here, dot_nt(pan[4, :, where], across))
+            accumulate(11, here, half_rows(0), dot_nt(along, pan[5, half_rows(0), where]))
 
     def far_first(kk, carry):
         far(0, kk)
@@ -284,10 +278,10 @@
         return carry
 
     lax.fori_loop(0, 4, far_second, 0)
-    for c in range(AHEAD, 4):
-        start(hops_corner(c))
     ship(FAR, 1)
     ship(LAST, WHOLE)
+    for c in range(EARLY, 4):
+        start(hops_corner(c))
 
     def corner(h, i):
         landed(hops_corner(2 * h + i))
@@ -297,16 +291,17 @@
             left = PAIRS[n][0]
             prod = dot_nt(pan[left, :, wide(i)], low)
             prod += dot_nt(pan[left, :, wide(2 + i)], high)
-            accumulate(n, everything, here, prod, i == 0)
-
-    for h in range(2):
-        for i in range(2):
-            corner(h, i)
-            if 2 * h + i == PASS_LAST:
-                pass_on(FAR, 1)
-                pass_on(LAST, WHOLE)
-        ship(CORNER, h)
+            accumulate(n, everything, here, prod)
+
+    corner(0, 0)
+    corner(0, 1)
+    ship(CORNER, 0)
+    pass_on(FAR, 1)
+    pass_on(LAST, WHOLE)
+    corner(1, 0)
+    corner(1, 1)
     pass_on(CORNER, 0)
+    ship(CORNER, 1)
     pass_on(CORNER, 1)
 
     def drain(k, carry):
@@ -355,42 +350,27 @@
             pltpu.SemaphoreType.DMA((8, 2)),
         ],
         compiler_params=pltpu.CompilerParams(
-            collective_id=0, has_side_effects=True, vmem_limit_bytes=59 * 2**20
+            collective_id=0, has_side_effects=True, vmem_limit_bytes=40 * 2**20
         ),
         name="meet",
     )(panel, sizes, signs)
 
 
-def place_kernel(blocks_in, front, tiles_in, out, blocks, total, tiles, blocks_sem, front_sem, tiles_sem, out_sem):
+def place_kernel(blocks, front, tiles, out, total, out_sem):
     group = lax.axis_index("group")
     member = lax.axis_index("member")
     width = 4 * B
 
-    def load_front(j):
-        return pltpu.make_async_copy(
-            front.at[:, j * width:(j + 1) * width], total.at[:, j * width:(j + 1) * width], front_sem.at[j]
-        )
-
-    def load_tile(g, j):
-        return pltpu.make_async_copy(tiles_in.at[g, j], tiles.at[g, j], tiles_sem.at[g, j])
-
     def store(j):
         return pltpu.make_async_copy(
             total.at[:, j * width:(j + 1) * width], out.at[:, j * width:(j + 1) * width], out_sem.at[j]
         )
 
-    load_blocks = pltpu.make_async_copy(blocks_in, blocks, blocks_sem)
-    load_blocks.start()
-    for j in range(2):
-        load_front(j).start()
-        for g in range(8):
-            load_tile(g, j).start()
-    load_blocks.wait()
     for j in range(2):
         run = 2 * group + j
-        load_front(j).wait()
+        side = slice(j * width, (j + 1) * width)
+        total[:, side] = front[:, side]
         for g in range(8):
-            load_tile(g, j).wait()
             for a in range(2):
                 r = blocks[g, 2 * member + a] - SIDE * member
                 for b in range(2):
@@ -406,24 +386,24 @@
     return pl.pallas_call(
         place_kernel,
         out_shape=jax.ShapeDtypeStruct(front.shape, jnp.float32),
-        in_specs=[pl.BlockSpec(memory_space=pl.ANY)] * 3,
+        in_specs=[
+            pl.BlockSpec(memory_space=pltpu.SMEM),
+            pl.BlockSpec(memory_space=pltpu.VMEM),
+            pl.BlockSpec(memory_space=pltpu.VMEM),
+        ],
         out_specs=pl.BlockSpec(memory_space=pl.ANY),
         scratch_shapes=[
-            pltpu.SMEM(blocks.shape, jnp.int32),
             pltpu.VMEM(front.shape, jnp.float32),
-            pltpu.VMEM(tiles.shape, jnp.bfloat16),
-            pltpu.SemaphoreType.DMA,
-            pltpu.SemaphoreType.DMA((2,)),
-            pltpu.SemaphoreType.DMA((8, 2)),
             pltpu.SemaphoreType.DMA((2,)),
         ],
-        compiler_params=pltpu.CompilerParams(vmem_limit_bytes=62 * 2**20),
+        compiler_params=pltpu.CompilerParams(vmem_limit_bytes=32 * 2**20),
         name="place",
     )(blocks, front, tiles)
 
 
 def local(root_front, child_panels, pivot_sizes, pivot_signs, child_blocks):
-    tiles = meet(child_panels, pivot_sizes, pivot_signs)
+    kept = [pltpu.with_memory_space_constraint(x, pltpu.HBM) for x in (child_panels, pivot_sizes, pivot_signs)]
+    tiles = meet(*kept)
     return place(child_blocks, root_front, tiles)
 
 

time: 89.4 us -> 87.9 us (0.983)
  Pallas kernels: 89.1 us -> 87.5 us
    pallas_call x1, Pallas kernels: 3.88 us -> 2.59 us  [place(): pl.pallas_call(place_kernel, out_shape=jax.ShapeDtypeStruct(front.shape,...]
where the time goes in v4:
time: 87.9 us; the launch traced here: 87.5 us
  Pallas kernels  87.5 us (100%)
    pallas_call x1, Pallas kernels, meet(): pl.pallas_call(meet_kernel, out_shape=jax.ShapeDtypeStruct((8, 2, ROWS, R...  84.9 us
    pallas_call x1, Pallas kernels, place(): pl.pallas_call(place_kernel, out_shape=jax.ShapeDtypeStruct(front.shape,...  2.59 us

profile of v4, /device:TPU:7, one launch (start us, length us, event | category | flops | bytes accessed | tf_op | source)
XLA Modules:
  0.0 87.5 jit_solution(8495581164508738456)
XLA Ops:
  0.0 0.0 copy-start.1
  0.0 0.0 copy-start
  0.0 84.9 %meet.1.tiles = bf16[8,2,256,256]{3,2,1,0:T(8,128)(2,1)S(1)} custom-call(bf16[1,256,4096]{2,1,0:T(8,128)(2,1)} %panel.1, f32[1,4096]{1,0:T(1,128)} %sizes_in.1, s32[1,4096]{1,0:T(1,128)} %signs_in.1), custom_call_target="tpu_custom_call" | custom-call | tf_op jit(solution)/shard_map/meet/pallas_call | solution.py:331
  84.9 0.0 copy-done.1
  84.9 0.0 copy-done
  85.0 2.6 %place.1 = f32[512,1024]{1,0:T(8,128)} custom-call(s32[8,32]{1,0:T(8,128)S(1)} %copy-done.1, f32[512,1024]{1,0:T(8,128)S(1)} %copy-done, bf16[8,2,256,256]{3,2,1,0:T(8,128)(2,1)S(1)} %meet.1.tiles), custom_call_target="tpu_custom_call" | custom-call | tf_op jit(solution)/shard_map/place/pallas_call | solution.py:386
Async XLA Ops:
  0.0 84.9 %copy-start.1 = (s32[8,32]{1,0:T(8,128)S(1)}, s32[8,32]{1,0:T(8,128)}, u32[]{:S(2)}) copy-start(s32[8,32]{1,0:T(8,128)} %blocks.1) | copy-start | bytes 3076
  0.0 84.9 %copy-start = (f32[512,1024]{1,0:T(8,128)S(1)}, f32[512,1024]{1,0:T(8,128)}, u32[]{:S(2)}) copy-start(f32[512,1024]{1,0:T(8,128)} %front.1) | copy-start | bytes 6291460

commit v5 on v4

--- a/solution.py
+++ b/solution.py
@@ -25,10 +25,10 @@
 TILES = tuple((n, a, b, False) for n, (a, b) in enumerate(PAIRS) if n != 6) + tuple(
     (n, PAIRS[n][1], PAIRS[n][0], True) for n in (2, 3, 5, 6, 8)
 )
-NEAR, CORNER, FAR, LAST = (0, 1, 2, 3), (4, 5, 6), (7, 8, 9, 10), (11,)
+SELF, NEAR, CORNER, FAR, LAST = (0,), (1, 2, 3), (4, 5, 6), (7, 8, 9, 10), (11,)
 WHOLE = 2
 PASS_NEAR, PASS_FAR = 2, 2
-EARLY = 2
+EARLY = 3
 
 
 def dot_nt(left, right):
@@ -212,7 +212,6 @@
 
     def near(k, carry):
         own = signed(0, everything, cols(k))
-        accumulate(0, everything, everything, dot_nt(own, pan[0, :, cols(k)]))
         landed(hops_own(k))
 
         @pl.when(k + AHEAD < NC)
@@ -228,6 +227,12 @@
         accumulate(3, everything, everything, dot_nt(signed(2, everything, cols(k)), pan[1, :, cols(k)]))
         return carry
 
+    def self_product(k, carry):
+        accumulate(0, everything, everything, dot_nt(signed(0, everything, cols(k)), pan[0, :, cols(k)]))
+        return carry
+
+    lax.fori_loop(0, NC, self_product, 0)
+    ship(SELF, WHOLE)
     lax.fori_loop(0, NC, near, 0)
     ship(NEAR, WHOLE)
 
@@ -314,7 +319,7 @@
         for copy in hops_corner(c):
             copy.wait_send()
     for slot, (n, r, _, _) in enumerate(TILES):
-        for h in (WHOLE,) if n in NEAR + LAST else (0, 1):
+        for h in (WHOLE,) if n in SELF + NEAR + LAST else (0, 1):
             if r != 0:
                 relay(slot, h).wait_send()
 
@@ -356,7 +361,7 @@
     )(panel, sizes, signs)
 
 
-def place_kernel(blocks, front, tiles, out, total, out_sem):
+def place_kernel(blocks_in, front, tiles, out, blocks, total, blocks_sem, out_sem):
     group = lax.axis_index("group")
     member = lax.axis_index("member")
     width = 4 * B
@@ -366,10 +371,12 @@
             total.at[:, j * width:(j + 1) * width], out.at[:, j * width:(j + 1) * width], out_sem.at[j]
         )
 
+    load_blocks = pltpu.make_async_copy(blocks_in, blocks, blocks_sem)
+    load_blocks.start()
+    total[...] = front[...]
+    load_blocks.wait()
     for j in range(2):
         run = 2 * group + j
-        side = slice(j * width, (j + 1) * width)
-        total[:, side] = front[:, side]
         for g in range(8):
             for a in range(2):
                 r = blocks[g, 2 * member + a] - SIDE * member
@@ -387,13 +394,15 @@
         place_kernel,
         out_shape=jax.ShapeDtypeStruct(front.shape, jnp.float32),
         in_specs=[
-            pl.BlockSpec(memory_space=pltpu.SMEM),
+            pl.BlockSpec(memory_space=pl.ANY),
             pl.BlockSpec(memory_space=pltpu.VMEM),
             pl.BlockSpec(memory_space=pltpu.VMEM),
         ],
         out_specs=pl.BlockSpec(memory_space=pl.ANY),
         scratch_shapes=[
+            pltpu.SMEM(blocks.shape, jnp.int32),
             pltpu.VMEM(front.shape, jnp.float32),
+            pltpu.SemaphoreType.DMA,
             pltpu.SemaphoreType.DMA((2,)),
         ],
         compiler_params=pltpu.CompilerParams(vmem_limit_bytes=32 * 2**20),

time: 87.9 us -> 87.6 us (level)
  no operation moved by 1% of the time
where the time goes in v5:
time: 87.6 us; the launch traced here: 86.9 us
  Pallas kernels  86.9 us (99%)
    pallas_call x1, Pallas kernels, meet(): pl.pallas_call(meet_kernel, out_shape=jax.ShapeDtypeStruct((8, 2, ROWS, R...  84.4 us
    pallas_call x1, Pallas kernels, place(): pl.pallas_call(place_kernel, out_shape=jax.ShapeDtypeStruct(front.shape,...  2.42 us

profile of v5, /device:TPU:7, one launch (start us, length us, event | category | flops | bytes accessed | tf_op | source)
XLA Modules:
  0.0 86.9 jit_solution(1043826057206986894)
XLA Ops:
  0.0 0.0 copy-start.1
  0.0 0.0 copy-start
  0.0 84.4 %meet.1.tiles = bf16[8,2,256,256]{3,2,1,0:T(8,128)(2,1)S(1)} custom-call(bf16[1,256,4096]{2,1,0:T(8,128)(2,1)} %panel.1, f32[1,4096]{1,0:T(1,128)} %sizes_in.1, s32[1,4096]{1,0:T(1,128)} %signs_in.1), custom_call_target="tpu_custom_call" | custom-call | tf_op jit(solution)/shard_map/meet/pallas_call | solution.py:336
  84.5 0.0 copy-done.1
  84.5 0.0 copy-done
  84.5 2.4 %place.1 = f32[512,1024]{1,0:T(8,128)} custom-call(s32[8,32]{1,0:T(8,128)S(1)} %copy-done.1, f32[512,1024]{1,0:T(8,128)S(1)} %copy-done, bf16[8,2,256,256]{3,2,1,0:T(8,128)(2,1)S(1)} %meet.1.tiles), custom_call_target="tpu_custom_call" | custom-call | tf_op jit(solution)/shard_map/place/pallas_call | solution.py:393
Async XLA Ops:
  0.0 84.5 %copy-start.1 = (s32[8,32]{1,0:T(8,128)S(1)}, s32[8,32]{1,0:T(8,128)}, u32[]{:S(2)}) copy-start(s32[8,32]{1,0:T(8,128)} %blocks_in.1) | copy-start | bytes 3076
  0.0 84.5 %copy-start = (f32[512,1024]{1,0:T(8,128)S(1)}, f32[512,1024]{1,0:T(8,128)}, u32[]{:S(2)}) copy-start(f32[512,1024]{1,0:T(8,128)} %front.1) | copy-start | bytes 6291460

commit v6 on v5

--- a/solution.py
+++ b/solution.py
@@ -27,6 +27,8 @@
 )
 SELF, NEAR, CORNER, FAR, LAST = (0,), (1, 2, 3), (4, 5, 6), (7, 8, 9, 10), (11,)
 WHOLE = 2
+QUARTERS = (3, 4)
+LANE = (0, 1, 0, 1, 2)
 PASS_NEAR, PASS_FAR = 2, 2
 EARLY = 3
 
@@ -37,11 +39,17 @@
 
 def half_rows(h):
     return pl.ds(h * B if isinstance(h, int) else pl.multiple_of(h * B, B), B)
+
+
+def quarter(h):
+    return pl.ds(B + (h - QUARTERS[0]) * (B // 2), B // 2)
 
 
 def part(ref, flipped, h):
     if h == WHOLE:
         return ref
+    if h in QUARTERS:
+        return ref.at[quarter(h), :]
     return ref.at[half_rows(h), :] if flipped else ref.at[:, half_rows(h)]
 
 
@@ -112,10 +120,15 @@
         return hop(1, 4, rows, columns, f, to_back), hop(2, 5, rows, columns, f, to_across)
 
     def hops_corner(c):
-        h, i = c // 2, c % 2
+        if c < 2:
+            return (
+                hop(4, 3, half_rows(0), wide(c), c, to_back),
+                hop(0, 3, half_rows(0), wide(2 + c), 2 + c, to_ahead),
+            )
+        rows = quarter(QUARTERS[c - 2])
         return (
-            hop(4, 3, half_rows(h), wide(i), 4 * h + i, to_back),
-            hop(0, 3, half_rows(h), wide(2 + i), 4 * h + 2 + i, to_ahead),
+            hop(4, 3, rows, pl.ds(0, K // 2), 2 * c, to_back),
+            hop(0, 3, rows, pl.ds(K // 2, K // 2), 2 * c + 1, to_ahead),
         )
 
     def start(pair):
@@ -151,8 +164,8 @@
         return pltpu.make_async_remote_copy(
             src_ref=part(stage.at[slot], flipped, h),
             dst_ref=part(mine.at[slot], flipped, h),
-            send_sem=relay_send.at[slot, h % 2],
-            recv_sem=relay_recv.at[slot, h % 2],
+            send_sem=relay_send.at[slot, LANE[h]],
+            recv_sem=relay_recv.at[slot, LANE[h]],
             device_id={"group": group, "member": at(CROSS[r])},
             device_id_type=pl.DeviceIdType.MESH,
         )
@@ -168,7 +181,7 @@
         return pltpu.make_async_remote_copy(
             src_ref=part(mine.at[slot], flipped, h),
             dst_ref=part(arrived.at[group, side], flipped, h),
-            send_sem=tile_send.at[slot, h % 2],
+            send_sem=tile_send.at[slot, LANE[h]],
             recv_sem=tile_recv.at[group, side],
             device_id={"group": owner, "member": member},
             device_id_type=pl.DeviceIdType.MESH,
@@ -190,12 +203,21 @@
         def _():
             to_owner(slot, h).start()
 
+    everything = slice(None)
+
+    def parts_of(slot):
+        n, _, _, flipped = TILES[slot]
+        if n in SELF + NEAR + LAST:
+            return (WHOLE,)
+        return (0, *QUARTERS) if n in CORNER and flipped else (0, 1)
+
     def ship(products, h):
         for here in (False, True):
             for slot, (n, r, _, flipped) in enumerate(TILES):
-                if n not in products or here != (r == 0):
+                if n not in products or here != (r == 0) or h not in parts_of(slot):
                     continue
-                value = (acc[n] if h == WHOLE else acc[n, :, half_rows(h)]).astype(jnp.bfloat16)
+                columns = everything if h == WHOLE else quarter(h) if h in QUARTERS else half_rows(h)
+                value = acc[n, :, columns].astype(jnp.bfloat16)
                 part((mine if here else stage).at[slot], flipped, h)[...] = value.T if flipped else value
                 if here:
                     deliver(slot, h)
@@ -204,11 +226,9 @@
 
     def pass_on(products, h):
         for slot, (n, r, _, _) in enumerate(TILES):
-            if n in products and r != 0:
+            if n in products and r != 0 and h in parts_of(slot):
                 relay(slot, h).wait_recv()
                 deliver(slot, h)
-
-    everything = slice(None)
 
     def near(k, carry):
         own = signed(0, everything, cols(k))
@@ -244,9 +264,11 @@
         def _():
             start(hops_far(f + AHEAD))
 
-        @pl.when(jnp.logical_and(f + AHEAD >= NC, f + AHEAD < NC + EARLY))
-        def _():
-            start(hops_corner(f + AHEAD - NC))
+        for c in range(EARLY):
+
+            @pl.when(f + AHEAD == NC + c)
+            def _():
+                start(hops_corner(c))
 
         here, where = half_rows(h), wide(kk)
         along = signed(4, here, where)
@@ -288,25 +310,32 @@
     for c in range(EARLY, 4):
         start(hops_corner(c))
 
-    def corner(h, i):
-        landed(hops_corner(2 * h + i))
-        here = half_rows(h)
-        low, high = signed(3, here, wide(i)), signed(3, here, wide(2 + i))
+    def corner(c):
+        landed(hops_corner(c))
+        if c < 2:
+            here, sides = half_rows(0), (wide(c), wide(2 + c))
+        else:
+            here, sides = quarter(QUARTERS[c - 2]), (pl.ds(0, K // 2), pl.ds(K // 2, K // 2))
+        low, high = signed(3, here, sides[0]), signed(3, here, sides[1])
         for n in CORNER:
             left = PAIRS[n][0]
-            prod = dot_nt(pan[left, :, wide(i)], low)
-            prod += dot_nt(pan[left, :, wide(2 + i)], high)
+            prod = dot_nt(pan[left, :, sides[0]], low)
+            prod += dot_nt(pan[left, :, sides[1]], high)
             accumulate(n, everything, here, prod)
 
-    corner(0, 0)
-    corner(0, 1)
+    corner(0)
+    corner(1)
     ship(CORNER, 0)
     pass_on(FAR, 1)
     pass_on(LAST, WHOLE)
-    corner(1, 0)
-    corner(1, 1)
+    corner(2)
+    ship(CORNER, 3)
+    corner(3)
     pass_on(CORNER, 0)
+    ship(CORNER, 4)
     ship(CORNER, 1)
+    pass_on(CORNER, 3)
+    pass_on(CORNER, 4)
     pass_on(CORNER, 1)
 
     def drain(k, carry):
@@ -319,7 +348,7 @@
         for copy in hops_corner(c):
             copy.wait_send()
     for slot, (n, r, _, _) in enumerate(TILES):
-        for h in (WHOLE,) if n in SELF + NEAR + LAST else (0, 1):
+        for h in parts_of(slot):
             if r != 0:
                 relay(slot, h).wait_send()
 
@@ -349,9 +378,9 @@
             pltpu.SemaphoreType.DMA((2,)),
             pltpu.SemaphoreType.DMA((5, NC)),
             pltpu.SemaphoreType.DMA((5, NC)),
-            pltpu.SemaphoreType.DMA((16, 2)),
-            pltpu.SemaphoreType.DMA((16, 2)),
-            pltpu.SemaphoreType.DMA((16, 2)),
+            pltpu.SemaphoreType.DMA((16, 3)),
+            pltpu.SemaphoreType.DMA((16, 3)),
+            pltpu.SemaphoreType.DMA((16, 3)),
             pltpu.SemaphoreType.DMA((8, 2)),
         ],
         compiler_params=pltpu.CompilerParams(

time: 87.6 us -> 88.9 us (1.015)
  Pallas kernels: 86.9 us -> 88.4 us
    pallas_call x1, Pallas kernels: 84.4 us -> 86 us  [meet(): pl.pallas_call(meet_kernel, out_shape=jax.ShapeDtypeStruct((8, 2, ROWS, R...]
where the time goes in v6:
time: 88.9 us; the launch traced here: 88.4 us
  Pallas kernels  88.4 us (99%)
    pallas_call x1, Pallas kernels, meet(): pl.pallas_call(meet_kernel, out_shape=jax.ShapeDtypeStruct((8, 2, ROWS, R...  86 us
    pallas_call x1, Pallas kernels, place(): pl.pallas_call(place_kernel, out_shape=jax.ShapeDtypeStruct(front.shape,...  2.41 us

profile of v6, /device:TPU:7, one launch (start us, length us, event | category | flops | bytes accessed | tf_op | source)
XLA Modules:
  0.0 88.4 jit_solution(5765081444346815328)
XLA Ops:
  0.0 0.0 copy-start.1
  0.0 0.0 copy-start
  0.0 86.0 %meet.1.tiles = bf16[8,2,256,256]{3,2,1,0:T(8,128)(2,1)S(1)} custom-call(bf16[1,256,4096]{2,1,0:T(8,128)(2,1)} %panel.1, f32[1,4096]{1,0:T(1,128)} %sizes_in.1, s32[1,4096]{1,0:T(1,128)} %signs_in.1), custom_call_target="tpu_custom_call" | custom-call | tf_op jit(solution)/shard_map/meet/pallas_call | solution.py:365
  86.0 0.0 copy-done.1
  86.0 0.0 copy-done
  86.0 2.4 %place.1 = f32[512,1024]{1,0:T(8,128)} custom-call(s32[8,32]{1,0:T(8,128)S(1)} %copy-done.1, f32[512,1024]{1,0:T(8,128)S(1)} %copy-done, bf16[8,2,256,256]{3,2,1,0:T(8,128)(2,1)S(1)} %meet.1.tiles), custom_call_target="tpu_custom_call" | custom-call | tf_op jit(solution)/shard_map/place/pallas_call | solution.py:422
Async XLA Ops:
  0.0 86.0 %copy-start.1 = (s32[8,32]{1,0:T(8,128)S(1)}, s32[8,32]{1,0:T(8,128)}, u32[]{:S(2)}) copy-start(s32[8,32]{1,0:T(8,128)} %blocks_in.1) | copy-start | bytes 3076
  0.0 86.0 %copy-start = (f32[512,1024]{1,0:T(8,128)S(1)}, f32[512,1024]{1,0:T(8,128)}, u32[]{:S(2)}) copy-start(f32[512,1024]{1,0:T(8,128)} %front.1) | copy-start | bytes 6291460

commit v7 on v5

--- a/solution.py
+++ b/solution.py
@@ -301,9 +301,9 @@
     corner(0, 0)
     corner(0, 1)
     ship(CORNER, 0)
+    corner(1, 0)
     pass_on(FAR, 1)
     pass_on(LAST, WHOLE)
-    corner(1, 0)
     corner(1, 1)
     pass_on(CORNER, 0)
     ship(CORNER, 1)

time: 87.6 us -> 87.6 us (level)
  no operation moved by 1% of the time
where the time goes in v7:
time: 87.6 us; the launch traced here: 86.9 us
  Pallas kernels  86.8 us (99%)
    pallas_call x1, Pallas kernels, meet(): pl.pallas_call(meet_kernel, out_shape=jax.ShapeDtypeStruct((8, 2, ROWS, R...  84.4 us
    pallas_call x1, Pallas kernels, place(): pl.pallas_call(place_kernel, out_shape=jax.ShapeDtypeStruct(front.shape,...  2.41 us

profile of v7, /device:TPU:7, one launch (start us, length us, event | category | flops | bytes accessed | tf_op | source)
XLA Modules:
  0.0 86.9 jit_solution(5429115531925352048)
XLA Ops:
  0.0 0.0 copy-start.1
  0.0 0.0 copy-start
  0.0 84.4 %meet.1.tiles = bf16[8,2,256,256]{3,2,1,0:T(8,128)(2,1)S(1)} custom-call(bf16[1,256,4096]{2,1,0:T(8,128)(2,1)} %panel.1, f32[1,4096]{1,0:T(1,128)} %sizes_in.1, s32[1,4096]{1,0:T(1,128)} %signs_in.1), custom_call_target="tpu_custom_call" | custom-call | tf_op jit(solution)/shard_map/meet/pallas_call | solution.py:336
  84.5 0.0 copy-done.1
  84.5 0.0 copy-done
  84.5 2.4 %place.1 = f32[512,1024]{1,0:T(8,128)} custom-call(s32[8,32]{1,0:T(8,128)S(1)} %copy-done.1, f32[512,1024]{1,0:T(8,128)S(1)} %copy-done, bf16[8,2,256,256]{3,2,1,0:T(8,128)(2,1)S(1)} %meet.1.tiles), custom_call_target="tpu_custom_call" | custom-call | tf_op jit(solution)/shard_map/place/pallas_call | solution.py:393
Async XLA Ops:
  0.0 84.5 %copy-start.1 = (s32[8,32]{1,0:T(8,128)S(1)}, s32[8,32]{1,0:T(8,128)}, u32[]{:S(2)}) copy-start(s32[8,32]{1,0:T(8,128)} %blocks_in.1) | copy-start | bytes 3076
  0.0 84.5 %copy-start = (f32[512,1024]{1,0:T(8,128)S(1)}, f32[512,1024]{1,0:T(8,128)}, u32[]{:S(2)}) copy-start(f32[512,1024]{1,0:T(8,128)} %front.1) | copy-start | bytes 6291460
